TPU v7x, 32 devices: a whole 2x2x4 slice. The times are simulated.
32 devices in a mesh: ctx: 8 (over z, y), kv: 4 (over x, core).
Axes of the slice: x: 2, y: 2, z: 4, core: 2. Of those that a mesh axis runs over, the one named last changes fastest.
Arguments:
- tokens: bfloat16 [4096, 8192], P('ctx', 'kv'), may hold values from -6 to 6
- segment_ids: int32 [4096], replicated, may hold values from 0 to 15, never falling along the last dimension, each value on 1 to 1024 neighbouring positions
- query_weight: bfloat16 [8192, 4096], P('ctx', 'kv'), may hold values from -2 to 2
- key_weight: bfloat16 [8192, 512], P('ctx', 'kv'), may hold values from -2 to 2
- value_projection_matrix: bfloat16 [8192, 512], P('ctx', 'kv'), may hold values from -0.0625 to 0.0625
Outputs:
- attended: bfloat16 [4096, 4096], P('ctx', 'kv')
Inputs may be any that keep to these rules, and one draw needn't show every extreme that they name: `segment_ids`: segment ids never fall along the sequence; each document holds 1 to 1024 tokens and one holds exactly 1024.
All inputs are finite; a program needn't handle non-finite values.
Results may differ from a plain program's by a relative error of at most 0.0085.
Values may be sent and summed in bfloat16 or wider, within the bound.
A program may use at most 128 MiB of HBM per device.

v0:
```python
import jax
import jax.numpy as jnp
from jax import lax
from jax.sharding import PartitionSpec as P

HEAD_DIMENSION = 128


def shifted(shard, axis, by):
    length = lax.axis_size(axis)
    pairs = [(i, i + by) for i in range(length) if 0 <= i + by < length]
    return lax.ppermute(shard, axis, pairs)


def attend_block(query_matrix, key_matrix, value_matrix, visible):
    head_size = query_matrix.shape[-1]
    scores = jnp.einsum(
        "thgd,shd->hgts", query_matrix, key_matrix, preferred_element_type=jnp.float32
    ) * head_size ** (-0.5)
    scores = jnp.where(visible[None, None], scores, -1e30)
    largest = jnp.max(scores, axis=-1, keepdims=True)
    expon = jnp.where(visible[None, None], jnp.exp(scores - largest), 0.0)
    total = jnp.sum(expon, axis=-1, keepdims=True)
    weights = expon.astype(jnp.bfloat16)
    summed = jnp.einsum("hgts,shd->hgtd", weights, value_matrix, preferred_element_type=jnp.float32)
    result = summed / total
    rows = query_matrix.shape[0]
    return jnp.transpose(result, (2, 0, 1, 3)).reshape(rows, -1).astype(jnp.bfloat16)


def shards(tokens, segment_ids, query_weight, key_weight, value_projection_matrix):
    whole = lax.all_gather(tokens, "kv", axis=1, tiled=True)
    rows = whole.shape[0]

    def add_rows(piece):
        return jnp.dot(whole, piece, preferred_element_type=jnp.float32)

    q_sum = add_rows(lax.all_gather(query_weight, "ctx", axis=0, tiled=True))
    k_sum = add_rows(lax.all_gather(key_weight, "ctx", axis=0, tiled=True))
    v_sum = add_rows(lax.all_gather(value_projection_matrix, "ctx", axis=0, tiled=True))
    query_rows = q_sum.astype(jnp.bfloat16)
    key_rows = k_sum.astype(jnp.bfloat16)
    value_rows = v_sum.astype(jnp.bfloat16)
    prev_key, prev_value = shifted((key_rows, value_rows), "ctx", 1)
    kv_heads = key_weight.shape[1] // HEAD_DIMENSION
    query_group = query_weight.shape[1] // (HEAD_DIMENSION * kv_heads)
    query_matrix = query_rows.reshape(rows, kv_heads, query_group, HEAD_DIMENSION)
    nearby_keys = jnp.concatenate([prev_key, key_rows], axis=0).reshape(
        2 * rows, kv_heads, HEAD_DIMENSION
    )
    nearby_values = jnp.concatenate([prev_value, value_rows], axis=0).reshape(
        2 * rows, kv_heads, HEAD_DIMENSION
    )
    position = lax.axis_index("ctx")
    begin_offset = position * rows
    prev_start = jnp.maximum(begin_offset - rows, 0)
    seg_query = lax.dynamic_slice_in_dim(segment_ids, begin_offset, rows, 0)
    seg_prev = lax.dynamic_slice_in_dim(segment_ids, prev_start, rows, 0)
    seg_keys = jnp.concatenate([seg_prev, seg_query], axis=0)
    qpos = begin_offset + jnp.arange(rows, dtype=jnp.int32)
    kpos = begin_offset - rows + jnp.arange(2 * rows, dtype=jnp.int32)
    visible = (kpos[None, :] <= qpos[:, None]) & (kpos[None, :] > qpos[:, None] - rows)
    visible = visible & (kpos[None, :] >= 0) & (seg_keys[None, :] == seg_query[:, None])
    return attend_block(query_matrix, nearby_keys, nearby_values, visible)


def solution(mesh):
    placed = (P("ctx", "kv"), P(), P("ctx", "kv"), P("ctx", "kv"), P("ctx", "kv"))
    return jax.shard_map(
        shards, mesh=mesh, in_specs=placed, out_specs=P("ctx", "kv"), check_vma=False
    )
```

profile of v0, /device:TPU:0, one launch (start us, length us, event | category | flops | bytes accessed | tf_op | source)
XLA Modules:
  0.0 434.3 jit_solution(8953648349559909561)
XLA Ops:
  6.5 0.0 all-gather.11.cloned.1.call-start
  6.5 0.7 all-gather.11.cloned.1.call-update
  7.3 0.0 all-gather.5.cloned.1.call-start
  7.3 0.7 all-gather.5.cloned.1.call-update
  8.0 0.0 all-gather.7.cloned.1.call-start
  8.1 0.7 all-gather.7.cloned.1.call-update
  8.7 0.0 all-gather.9.cloned.1.call-start
  8.8 0.5 all-gather.9.cloned.1.call-update
  9.3 0.8 fusion.22
  10.2 1.0 compare_and_fusion
  11.2 50.3 %all-gather.11.cloned.1.call-done = bf16[8192,128]{1,0:T(8,128)(2,1)} async-done(((bf16[1024,128]{1,0:T(8,128)(2,1)}), bf16[8192,128]{1,0:T(8,128)(2,1)}) %all-gather.11.cloned.1.call-update) | async-done | bytes 2097168 | tf_op jit(solution)/shard_map/all_gather | solution.py:40
  61.5 58.4 %all-gather.5.cloned.1.call-done = bf16[512,8192]{1,0:T(8,128)(2,1)} async-done(((bf16[512,2048]{1,0:T(8,128)(2,1)}), bf16[512,8192]{1,0:T(8,128)(2,1)}) %all-gather.5.cloned.1.call-update) | async-done | bytes 8388624 | tf_op jit(solution)/shard_map/all_gather | solution.py:32
  119.9 6.3 %convolution_convert_fusion.1 = bf16[512,128]{1,0:T(8,128)(2,1)S(1)} fusion(bf16[512,8192]{1,0:T(8,128)(2,1)} %all-gather.5.cloned.1.call-done, bf16[8192,128]{1,0:T(8,128)(2,1)} %all-gather.11.cloned.1.call-done), kind=kOutput, calls=%fused_computation.12 | convolution fusion | flops 1073807360 | bytes 10616832 | tf_op jit(solution)/shard_map/dot_general | solution.py:36
  126.2 3.4 collective-permute-start.1
  129.6 42.6 %all-gather.7.cloned.1.call-done = bf16[8192,128]{1,0:T(8,128)(2,1)} async-done(((bf16[1024,128]{1,0:T(8,128)(2,1)}), bf16[8192,128]{1,0:T(8,128)(2,1)}) %all-gather.7.cloned.1.call-update) | async-done | bytes 2097168 | tf_op jit(solution)/shard_map/all_gather | solution.py:39
  172.2 6.3 %convolution_convert_fusion.2 = bf16[512,128]{1,0:T(8,128)(2,1)S(1)} fusion(bf16[512,8192]{1,0:T(8,128)(2,1)} %all-gather.5.cloned.1.call-done, bf16[8192,128]{1,0:T(8,128)(2,1)} %all-gather.7.cloned.1.call-done), kind=kOutput, calls=%fused_computation.13 | convolution fusion | flops 1073807360 | bytes 10616832 | tf_op jit(solution)/shard_map/dot_general | solution.py:36
  178.5 2.6 collective-permute-start
  181.1 219.3 %all-gather.9.cloned.1.call-done = bf16[8192,1024]{1,0:T(8,128)(2,1)} async-done(((bf16[1024,1024]{1,0:T(8,128)(2,1)}), bf16[8192,1024]{1,0:T(8,128)(2,1)}) %all-gather.9.cloned.1.call-update) | async-done | bytes 16777232 | tf_op jit(solution)/shard_map/all_gather | solution.py:38
  400.4 14.8 %fusion.7 = bf16[64,8,8,128]{3,2,1,0:T(8,128)(2,1)S(1)} fusion(bf16[512,8192]{1,0:T(8,128)(2,1)} %all-gather.5.cloned.1.call-done, bf16[8192,1024]{1,0:T(8,128)(2,1)} %all-gather.9.cloned.1.call-done), kind=kOutput, calls=%fused_computation.11 | convolution fusion | flops 8590458880 | bytes 26214400 | tf_op jit(solution)/shard_map/dot_general | solution.py:36
  415.1 0.0 collective-permute-done
  415.2 2.9 fusion
  418.1 4.0 fusion.1
  422.1 0.0 collective-permute-done.1
  422.1 4.3 divide_convert_fusion
  426.4 1.3 copy.9
  (3 shorter events, 0.0 us)
Async XLA Ops:
  6.5 55.0 %all-gather.11.cloned.1.call-start = ((), (), s32[]{:S(2)}) async-start(), calls=%async_computation.3 | async-start | bytes 2359296 | tf_op jit(solution)/shard_map/all_gather | solution.py:40
  7.3 112.6 %all-gather.5.cloned.1.call-start = ((), (), s32[]{:S(2)}) async-start(), calls=%async_computation | async-start | bytes 10485760 | tf_op jit(solution)/shard_map/all_gather | solution.py:32
  8.0 164.1 %all-gather.7.cloned.1.call-start = ((), (), s32[]{:S(2)}) async-start(), calls=%async_computation.1 | async-start | bytes 2359296 | tf_op jit(solution)/shard_map/all_gather | solution.py:39
  8.7 391.6 %all-gather.9.cloned.1.call-start = ((), (), s32[]{:S(2)}) async-start(), calls=%async_computation.2 | async-start | bytes 18874368 | tf_op jit(solution)/shard_map/all_gather | solution.py:38
  126.2 295.9 %collective-permute-start.1 = (bf16[512,128]{1,0:T(8,128)(2,1)S(1)}, bf16[512,128]{1,0:T(8,128)(2,1)S(1)}, u32[]{:S(2)}, u32[]{:S(2)}) collective-permute-start(bf16[512,128]{1,0:T(8,128)(2,1)S(1)} %convolution_convert_fusion.1), channel_id=1, source_target_pairs={{0,4},{4,8},{8,12},{12,16},{16,20},{20,24},{24,28},{1,5},{5,9},{9,... | collective-permute-start | bytes 393224 | tf_op jit(solution)/shard_map/ppermute | solution.py:12
  178.5 236.7 %collective-permute-start = (bf16[512,128]{1,0:T(8,128)(2,1)S(1)}, bf16[512,128]{1,0:T(8,128)(2,1)S(1)}, u32[]{:S(2)}, u32[]{:S(2)}) collective-permute-start(bf16[512,128]{1,0:T(8,128)(2,1)S(1)} %convolution_convert_fusion.2), channel_id=1, source_target_pairs={{0,4},{4,8},{8,12},{12,16},{16,20},{20,24},{24,28},{1,5},{5,9},{9,... | collective-permute-start | bytes 393224 | tf_op jit(solution)/shard_map/ppermute | solution.py:12
Sparse Core Ops, SparseCore 0:
  9.5 51.9 all-gather.10
  63.1 56.7 all-gather.4
  122.0 50.1 all-gather.6
  174.1 226.1 all-gather.8
where the time goes:
time: 435 us; the launch traced here: 434 us
  waiting for transfers between devices  373 us (86%)
  matrix products  34.6 us (8%)
  between operations  13.2 us (3%)
  starting transfers between devices  6.15 us (1%)
  other arithmetic  5.01 us (1%)
    all_gather x1, waiting for transfers between devices, shards(): q_sum = add_rows(lax.all_gather(query_weight, 'ctx', axis=0, tiled=True))  219 us
    all_gather x1, waiting for transfers between devices, shards(): whole = lax.all_gather(tokens, 'kv', axis=1, tiled=True)  58.4 us
    all_gather x1, waiting for transfers between devices, shards(): lax.all_gather(value_projection_matrix, 'ctx', axis=0, tiled=True)  50.3 us
    all_gather x1, waiting for transfers between devices, shards(): k_sum = add_rows(lax.all_gather(key_weight, 'ctx', axis=0, tiled=True))  42.6 us
    dot_general x3, matrix products, add_rows(): return jnp.dot(whole, piece, preferred_element_type=jnp.float32)  27.4 us
  transfers between devices with their start and end apart: 6, of which 4 were waited for; matrix products, arithmetic and copies ran while one was open for 8% of the time, Pallas kernels for 0%

commit v1 on v0

--- a/solution.py
+++ b/solution.py
@@ -2,6 +2,7 @@
 import jax.numpy as jnp
 from jax import lax
 from jax.sharding import PartitionSpec as P
+from jax.lax import axis_index, axis_size, ppermute
 
 HEAD_DIMENSION = 128
 
@@ -29,6 +30,30 @@
 
 
 def shards(tokens, segment_ids, query_weight, key_weight, value_projection_matrix):
+
+    def pack_sectors(z):
+        tmp, left_arr, spare = (axis_size("ctx"), axis_index("ctx"), z.shape[0])
+        sides = [j0 * tmp if w == 0 else j0 for w, j0 in enumerate(z.shape)]
+        tile_out = lax.dynamic_update_slice_in_dim(
+            jnp.zeros(sides, z.dtype), z, left_arr * spare, axis=0
+        )
+        b_now = r1 = z
+        for s in range(1, tmp // 2 + 1):
+            b_now = ppermute(
+                b_now, axis_name="ctx", perm=list(map(lambda w: (w, (w + 1) % tmp), range(tmp)))
+            )
+            tile_out = lax.dynamic_update_slice_in_dim(
+                tile_out, b_now, (left_arr - s) % tmp * spare, axis=0
+            )
+            if 2 * s < tmp:
+                r1 = ppermute(
+                    r1, axis_name="ctx", perm=list(map(lambda w: (w, (w - 1) % tmp), range(tmp)))
+                )
+                tile_out = lax.dynamic_update_slice_in_dim(
+                    tile_out, r1, (left_arr + s) % tmp * spare, axis=0
+                )
+        return tile_out
+
     whole = lax.all_gather(tokens, "kv", axis=1, tiled=True)
     rows = whole.shape[0]
 
@@ -37,7 +62,7 @@
 
     q_sum = add_rows(lax.all_gather(query_weight, "ctx", axis=0, tiled=True))
     k_sum = add_rows(lax.all_gather(key_weight, "ctx", axis=0, tiled=True))
-    v_sum = add_rows(lax.all_gather(value_projection_matrix, "ctx", axis=0, tiled=True))
+    v_sum = add_rows(pack_sectors(value_projection_matrix))
     query_rows = q_sum.astype(jnp.bfloat16)
     key_rows = k_sum.astype(jnp.bfloat16)
     value_rows = v_sum.astype(jnp.bfloat16)

time: 435 us -> 407 us (0.936)
  waiting for transfers between devices: 373 us -> 326 us
  starting transfers between devices: 6.15 us -> 25.3 us
    all_gather x1 -> x0, waiting for transfers between devices: 50.3 us -> none  [shards(): lax.all_gather(value_projection_matrix, 'ctx', axis=0, tiled=True)]
    ppermute x0 -> x7, waiting for transfers between devices: none -> 41 us  [the longest x4 40.6 us: pack_sectors(): ppermute(b_now, axis_name='ctx', perm=list(map(lambda w: (w, (w + 1) % tm...]
    all_gather x1, waiting for transfers between devices: 42.6 us -> 6.69 us  [shards(): k_sum = add_rows(lax.all_gather(key_weight, 'ctx', axis=0, tiled=True))]
    ppermute x0 -> x7, starting transfers between devices: none -> 18.3 us  [the longest x3 11.7 us: pack_sectors(): ppermute(r1, axis_name='ctx', perm=list(map(lambda w: (w, (w - 1) % tmp),...]
  transfers between devices with their start and end apart: 6 -> 12, of which waited for: 4 -> 8; matrix products, arithmetic and copies ran while one was open for 8% -> 9% of each run, Pallas kernels for 0% -> 0%
where the time goes in v1:
time: 407 us; the launch traced here: 406 us
  waiting for transfers between devices  326 us (80%)
  matrix products  32.1 us (8%)
  starting transfers between devices  25.3 us (6%)
  between operations  13.4 us (3%)
  other arithmetic  4.98 us (1%)
  local copies, waits for them, and re-layouts  4.65 us (1%)
    all_gather x1, waiting for transfers between devices, shards(): q_sum = add_rows(lax.all_gather(query_weight, 'ctx', axis=0, tiled=True))  216 us
    all_gather x1, waiting for transfers between devices, shards(): whole = lax.all_gather(tokens, 'kv', axis=1, tiled=True)  60 us
    ppermute x4, waiting for transfers between devices, pack_sectors(): ppermute(b_now, axis_name='ctx', perm=list(map(lambda w: (w, (w + 1) % tm...  40.6 us
    dot_general x3, matrix products, add_rows(): return jnp.dot(whole, piece, preferred_element_type=jnp.float32)  24.2 us
    ppermute x3, starting transfers between devices, pack_sectors(): ppermute(r1, axis_name='ctx', perm=list(map(lambda w: (w, (w - 1) % tmp),...  11.7 us
  transfers between devices with their start and end apart: 12, of which 8 were waited for; matrix products, arithmetic and copies ran while one was open for 9% of the time, Pallas kernels for 0%

profile of v1, /device:TPU:0, one launch (start us, length us, event | category | flops | bytes accessed | tf_op | source)
XLA Modules:
  0.0 406.3 jit_solution(5667215179190038981)
XLA Ops:
  6.5 0.7 all-gather.6.cloned.1.call-update
  7.3 0.7 all-gather.4.cloned.1.call-update
  8.0 0.0 all-gather.8.cloned.1.call-start
  8.1 0.7 all-gather.8.cloned.1.call-update
  8.8 6.1 %collective-permute-start.2 = (bf16[1024,128]{1,0:T(8,128)(2,1)S(1)}, bf16[1024,128]{1,0:T(8,128)(2,1)S(1)}, u32[]{:S(2)}, u32[]{:S(2)}) collective-permute-start(bf16[1024,128]{1,0:T(8,128)(2,1)S(1)} %copy-done.1), channel_id=1, source_target_pairs={{0,28},{4,0},{8,4},{12,8},{16,12},{20,16},{24,20},{28,24},{1,29},{... | collective-permute-start | bytes 786440 | tf_op jit(solution)/shard_map/ppermute | solution.py:49
  14.8 0.8 fusion.23
  15.7 11.0 %collective-permute-done.1 = bf16[1024,128]{1,0:T(8,128)(2,1)S(1)} collective-permute-done((bf16[1024,128]{1,0:T(8,128)(2,1)S(1)}, bf16[1024,128]{1,0:T(8,128)(2,1)S(1)}, u32[]{:S(2)}, u32[]{:S(2)}) %collective-permute-start.1) | collective-permute-done | bytes 262176 | tf_op jit(solution)/shard_map/ppermute | solution.py:42
  26.7 2.5 collective-permute-start.3
  29.1 0.9 compare_and_fusion
  30.1 3.0 collective-permute-start.4
  33.1 0.3 broadcast_in_dim.35
  33.5 7.9 %collective-permute-done.3 = bf16[1024,128]{1,0:T(8,128)(2,1)} collective-permute-done((bf16[1024,128]{1,0:T(8,128)(2,1)S(1)}, bf16[1024,128]{1,0:T(8,128)(2,1)}, u32[]{:S(2)}, u32[]{:S(2)}) %collective-permute-start.3) | collective-permute-done | bytes 262176 | tf_op jit(solution)/shard_map/ppermute | solution.py:42
  41.5 1.7 collective-permute-start.5
  43.3 0.4 collective-permute-done.4
  43.6 2.7 collective-permute-start.6
  46.3 1.0 constant_dynamic-update-slice_fusion.4
  47.3 13.3 %collective-permute-done.5 = bf16[1024,128]{1,0:T(8,128)(2,1)S(1)} collective-permute-done((bf16[1024,128]{1,0:T(8,128)(2,1)}, bf16[1024,128]{1,0:T(8,128)(2,1)S(1)}, u32[]{:S(2)}, u32[]{:S(2)}) %collective-permute-start.5) | collective-permute-done | bytes 262176 | tf_op jit(solution)/shard_map/ppermute | solution.py:42
  60.6 2.4 collective-permute-start.7
  62.9 1.0 constant_dynamic-update-slice_fusion.3
  64.0 8.5 %collective-permute-done.7 = bf16[1024,128]{1,0:T(8,128)(2,1)S(1)} collective-permute-done((bf16[1024,128]{1,0:T(8,128)(2,1)S(1)}, bf16[1024,128]{1,0:T(8,128)(2,1)S(1)}, u32[]{:S(2)}, u32[]{:S(2)}) %collective-permute-start.7) | collective-permute-done | bytes 262176 | tf_op jit(solution)/shard_map/ppermute | solution.py:42
  72.5 6.7 %all-gather.6.cloned.1.call-done = bf16[8192,128]{1,0:T(8,128)(2,1)} async-done(((bf16[1024,128]{1,0:T(8,128)(2,1)}), bf16[8192,128]{1,0:T(8,128)(2,1)}) %all-gather.6.cloned.1.call-update) | async-done | bytes 2097168 | tf_op jit(solution)/shard_map/all_gather | solution.py:64
  79.2 60.0 %all-gather.4.cloned.1.call-done = bf16[512,8192]{1,0:T(8,128)(2,1)} async-done(((bf16[512,2048]{1,0:T(8,128)(2,1)}), bf16[512,8192]{1,0:T(8,128)(2,1)}) %all-gather.4.cloned.1.call-update) | async-done | bytes 8388624 | tf_op jit(solution)/shard_map/all_gather | solution.py:57
  139.2 6.4 %convolution_convert_fusion.2 = bf16[512,128]{1,0:T(8,128)(2,1)S(1)} fusion(bf16[512,8192]{1,0:T(8,128)(2,1)} %all-gather.4.cloned.1.call-done, bf16[8192,128]{1,0:T(8,128)(2,1)} %all-gather.6.cloned.1.call-done), kind=kOutput, calls=%fused_computation.13 | convolution fusion | flops 1073807360 | bytes 10616832 | tf_op jit(solution)/shard_map/dot_general | solution.py:61
  145.7 3.4 collective-permute-start
  149.1 2.9 fusion.8
  152.0 3.6 collective-permute-start.8
  155.6 216.0 %all-gather.8.cloned.1.call-done = bf16[8192,1024]{1,0:T(8,128)(2,1)} async-done(((bf16[1024,1024]{1,0:T(8,128)(2,1)}), bf16[8192,1024]{1,0:T(8,128)(2,1)}) %all-gather.8.cloned.1.call-update) | async-done | bytes 16777232 | tf_op jit(solution)/shard_map/all_gather | solution.py:63
  371.6 14.8 %fusion.7 = bf16[64,8,8,128]{3,2,1,0:T(8,128)(2,1)S(1)} fusion(bf16[512,8192]{1,0:T(8,128)(2,1)} %all-gather.4.cloned.1.call-done, bf16[8192,1024]{1,0:T(8,128)(2,1)} %all-gather.8.cloned.1.call-done), kind=kOutput, calls=%fused_computation.11 | convolution fusion | flops 8590458880 | bytes 26214400 | tf_op jit(solution)/shard_map/dot_general | solution.py:61
  386.4 2.9 fusion
  389.3 4.0 fusion.1
  393.4 5.0 %divide_convert_fusion = bf16[8,512,128]{1,2,0:T(8,128)(2,1)S(1)} fusion(f32[8,512]{1,0:T(8,128)S(1)} %fusion.1, f32[1024,512,8]{1,0,2:T(8,128)S(1)} %get-tuple-element.8, f32[8,512]{1,0:T(8,128)S(1)} %get-tuple-element.7, pred[512,1024]{0,1:T(8,128)(4,1)S(1)} %compare_and_fusion, bf16[512,128]{0,1:T(8,128)(2,1)S(1)} %fusion.8, ...), kind=kOutput, calls=%fused_computation.8 | convolution fusion | flops 1096286208 | bytes 18644992 | tf_op jit(solution)/shard_map/hgts,shd->hgtd/dot_general | solution.py:26
  398.4 1.3 copy.8
  (20 shorter events, 0.3 us)
Async XLA Ops:
  6.5 2.2 copy-start.1
  6.5 72.7 %all-gather.6.cloned.1.call-start = ((), (), s32[]{:S(2)}) async-start(), calls=%async_computation.1 | async-start | bytes 2359296 | tf_op jit(solution)/shard_map/all_gather | solution.py:64
  7.3 131.9 %all-gather.4.cloned.1.call-start = ((), (), s32[]{:S(2)}) async-start(), calls=%async_computation | async-start | bytes 10485760 | tf_op jit(solution)/shard_map/all_gather | solution.py:57
  8.0 363.6 %all-gather.8.cloned.1.call-start = ((), (), s32[]{:S(2)}) async-start(), calls=%async_computation.2 | async-start | bytes 18874368 | tf_op jit(solution)/shard_map/all_gather | solution.py:63
  8.8 21.3 %collective-permute-start.2 = (bf16[1024,128]{1,0:T(8,128)(2,1)S(1)}, bf16[1024,128]{1,0:T(8,128)(2,1)S(1)}, u32[]{:S(2)}, u32[]{:S(2)}) collective-permute-start(bf16[1024,128]{1,0:T(8,128)(2,1)S(1)} %copy-done.1), channel_id=1, source_target_pairs={{0,28},{4,0},{8,4},{12,8},{16,12},{20,16},{24,20},{28,24},{1,29},{... | collective-permute-start | bytes 786440 | tf_op jit(solution)/shard_map/ppermute | solution.py:49
  14.8 11.9 %collective-permute-start.1 = (bf16[1024,128]{1,0:T(8,128)(2,1)S(1)}, bf16[1024,128]{1,0:T(8,128)(2,1)S(1)}, u32[]{:S(2)}, u32[]{:S(2)}) collective-permute-start(bf16[1024,128]{1,0:T(8,128)(2,1)S(1)} %copy-done.1), channel_id=1, source_target_pairs={{0,4},{4,8},{8,12},{12,16},{16,20},{20,24},{24,28},{28,0},{1,5},{5... | collective-permute-start | bytes 786440 | tf_op jit(solution)/shard_map/ppermute | solution.py:42
  26.7 14.8 %collective-permute-start.3 = (bf16[1024,128]{1,0:T(8,128)(2,1)S(1)}, bf16[1024,128]{1,0:T(8,128)(2,1)}, u32[]{:S(2)}, u32[]{:S(2)}) collective-permute-start(bf16[1024,128]{1,0:T(8,128)(2,1)S(1)} %collective-permute-done.1), channel_id=1, source_target_pairs={{0,4},{4,8},{8,12},{12,16},{16,20},{20,24},{24,28},{28,0},{1,5},{5... | collective-permute-start | bytes 786440 | tf_op jit(solution)/shard_map/ppermute | solution.py:42
  30.1 13.5 %collective-permute-start.4 = (bf16[1024,128]{1,0:T(8,128)(2,1)S(1)}, bf16[1024,128]{1,0:T(8,128)(2,1)}, u32[]{:S(2)}, u32[]{:S(2)}) collective-permute-start(bf16[1024,128]{1,0:T(8,128)(2,1)S(1)} %collective-permute-done.2), channel_id=1, source_target_pairs={{0,28},{4,0},{8,4},{12,8},{16,12},{20,16},{24,20},{28,24},{1,29},{... | collective-permute-start | bytes 786440 | tf_op jit(solution)/shard_map/ppermute | solution.py:49
  41.5 19.1 %collective-permute-start.5 = (bf16[1024,128]{1,0:T(8,128)(2,1)}, bf16[1024,128]{1,0:T(8,128)(2,1)S(1)}, u32[]{:S(2)}, u32[]{:S(2)}) collective-permute-start(bf16[1024,128]{1,0:T(8,128)(2,1)} %collective-permute-done.3), channel_id=1, source_target_pairs={{0,4},{4,8},{8,12},{12,16},{16,20},{20,24},{24,28},{28,0},{1,5},{5... | collective-permute-start | bytes 786440 | tf_op jit(solution)/shard_map/ppermute | solution.py:42
  43.6 20.4 %collective-permute-start.6 = (bf16[1024,128]{1,0:T(8,128)(2,1)}, bf16[1024,128]{1,0:T(8,128)(2,1)S(1)}, u32[]{:S(2)}, u32[]{:S(2)}) collective-permute-start(bf16[1024,128]{1,0:T(8,128)(2,1)} %collective-permute-done.4), channel_id=1, source_target_pairs={{0,28},{4,0},{8,4},{12,8},{16,12},{20,16},{24,20},{28,24},{1,29},{... | collective-permute-start | bytes 786440 | tf_op jit(solution)/shard_map/ppermute | solution.py:49
  60.6 11.9 %collective-permute-start.7 = (bf16[1024,128]{1,0:T(8,128)(2,1)S(1)}, bf16[1024,128]{1,0:T(8,128)(2,1)S(1)}, u32[]{:S(2)}, u32[]{:S(2)}) collective-permute-start(bf16[1024,128]{1,0:T(8,128)(2,1)S(1)} %collective-permute-done.5), channel_id=1, source_target_pairs={{0,4},{4,8},{8,12},{12,16},{16,20},{20,24},{24,28},{28,0},{1,5},{5... | collective-permute-start | bytes 786440 | tf_op jit(solution)/shard_map/ppermute | solution.py:42
  139.2 9.9 %copy-start = (bf16[512,8192]{1,0:T(8,128)(2,1)S(1)}, bf16[512,8192]{1,0:T(8,128)(2,1)}, u32[]{:S(2)}) copy-start(bf16[512,8192]{1,0:T(8,128)(2,1)} %all-gather.4.cloned.1.call-done) | copy-start | bytes 25165828
  145.7 240.7 %collective-permute-start = (bf16[512,128]{1,0:T(8,128)(2,1)S(1)}, bf16[512,128]{1,0:T(8,128)(2,1)S(1)}, u32[]{:S(2)}, u32[]{:S(2)}) collective-permute-start(bf16[512,128]{1,0:T(8,128)(2,1)S(1)} %convolution_convert_fusion.2), channel_id=1, source_target_pairs={{0,4},{4,8},{8,12},{12,16},{16,20},{20,24},{24,28},{1,5},{5,9},{9,... | collective-permute-start | bytes 393224 | tf_op jit(solution)/shard_map/ppermute | solution.py:13
  152.0 241.4 %collective-permute-start.8 = (bf16[512,128]{0,1:T(8,128)(2,1)S(1)}, bf16[512,128]{0,1:T(8,128)(2,1)S(1)}, u32[]{:S(2)}, u32[]{:S(2)}) collective-permute-start(bf16[512,128]{0,1:T(8,128)(2,1)S(1)} %fusion.8), channel_id=1, source_target_pairs={{0,4},{4,8},{8,12},{12,16},{16,20},{20,24},{24,28},{1,5},{5,9},{9,... | collective-permute-start | bytes 393224 | tf_op jit(solution)/shard_map/ppermute | solution.py:13
Sparse Core Ops, SparseCore 0:
  9.5 69.7 all-gather.5
  80.8 58.3 all-gather.3
  141.3 230.2 all-gather.7
